TPU v7x, 32 devices: a whole 2x2x4 slice. The times are simulated.
32 devices in a mesh: dom: 8 (over z, x), grp: 4 (over y, core).
Axes of the slice: x: 2, y: 2, z: 4, core: 2. Of those that a mesh axis runs over, the one named last changes fastest.
Arguments:
- blocks: bfloat16 [1536, 6, 128, 128], P(('dom', 'grp')), may hold values from -0.21875 to 0.21875
- local_cols: int32 [1536, 4], P(('dom', 'grp')), may hold values from 0 to 191
- remote_refs: int32 [1536, 2], P(('dom', 'grp')), may hold values from 0 to 23
- send_blocks: int32 [8, 4, 8, 3], P('dom', 'grp'), may hold values from 0 to 47
- send_counts: int32 [8, 4, 8], P('dom', 'grp'), may hold values from 0 to 3
- probes: bfloat16 [64, 196608], P(None, ('dom', 'grp')), may hold values from -6 to 6
Outputs:
- moments: float32 [3, 196608], P(None, ('dom', 'grp'))
All inputs are finite; a program needn't handle non-finite values.
Results may differ from a plain program's by a relative error of at most 0.00064.
Values may be sent and summed in bfloat16 or wider, within the bound.
A program may use at most 64 MiB of HBM per device.

v0:
```python
import math

import jax
import jax.numpy as jnp
from jax import lax
from jax.sharding import PartitionSpec as P

PROBES = 64
LOCAL = 4
KMOM = 256


def jackson(order, total):
    angle = math.pi / (total + 1)
    return (
        (total - order + 1) * math.cos(order * angle) + math.sin(order * angle) / math.tan(angle)
    ) / (total + 1)


def send_boundary(own, send_list, live):
    outgoing = jnp.take(own, send_list, axis=1)
    outgoing = jnp.where(live[None, :, :, None], outgoing, jnp.zeros_like(outgoing))
    received = lax.all_to_all(outgoing, "dom", split_axis=1, concat_axis=1, tiled=True)
    return received.reshape(own.shape[0], -1, own.shape[2])


def on_device(blocks, local_cols, remote_refs, send_blocks, send_counts, probes):
    rows_here = blocks.shape[0]
    size_block = blocks.shape[2]
    probe_count = probes.shape[0]
    local_blocks = blocks[:, :LOCAL]
    remote_blocks = blocks[:, LOCAL:]
    send_list = send_blocks[0, 0]
    slot_index = jnp.arange(send_list.shape[1], dtype=jnp.int32)
    live = slot_index[None, :] < send_counts[0, 0][:, None]

    def local_part(own):
        empty = jnp.zeros((probe_count, rows_here, LOCAL, size_block), jnp.bfloat16)
        piece = lax.all_gather(own, "grp", axis=1, tiled=True)
        start = jnp.int32(0)
        width = piece.shape[1]
        inside = (local_cols >= start) & (local_cols < start + width)
        index = jnp.clip(local_cols, 0, width - 1)
        chosen = jnp.take(piece, index, axis=1)
        picked = jnp.where(inside[None, :, :, None], chosen, empty)
        return jnp.einsum(
            "rjab,prjb->pra", local_blocks, picked, preferred_element_type=jnp.float32
        )

    def remote_part(received):
        picked = jnp.take(received, remote_refs, axis=1)
        return jnp.einsum(
            "rjab,prjb->pra", remote_blocks, picked, preferred_element_type=jnp.float32
        )

    def apply_op(field):
        own = field.reshape(probe_count, rows_here, size_block)
        local_sum = local_part(own)
        received = send_boundary(own, send_list, live)
        result = local_sum + remote_part(received)
        return result.reshape(probe_count, rows_here * size_block)

    first = apply_op(probes).astype(jnp.bfloat16)
    base = probes.astype(jnp.float32)
    second = 2.0 * apply_op(first) - base
    norm = 1.0 / math.sqrt(PROBES)
    moment_zero = jackson(0, KMOM) * norm * jnp.sum(base * base, axis=0)
    moment_one = 2.0 * jackson(1, KMOM) * norm * jnp.sum(base * first.astype(jnp.float32), axis=0)
    moment_two = 2.0 * jackson(2, KMOM) * norm * jnp.sum(base * second, axis=0)
    return jnp.stack([moment_zero, moment_one, moment_two], axis=0)


def solution(mesh):
    in_specs = (
        P(("dom", "grp"), None, None, None),
        P(("dom", "grp"), None),
        P(("dom", "grp"), None),
        P("dom", "grp", None, None),
        P("dom", "grp", None),
        P(None, ("dom", "grp")),
    )
    out_specs = P(None, ("dom", "grp"))
    return jax.shard_map(
        on_device, mesh=mesh, in_specs=in_specs, out_specs=out_specs, check_vma=False
    )
```

profile of v0, /device:TPU:0, one launch (start us, length us, event | category | flops | bytes accessed | tf_op | source)
XLA Modules:
  0.0 98.7 jit_solution(1945905450059347145)
XLA Ops:
  6.5 0.0 copy-start.3
  6.5 0.0 copy-start.5
  6.5 0.0 all-gather.3.cloned.1.call-start
  6.5 2.3 %copy_bitcast_fusion = bf16[64,48,128]{2,0,1:T(8,128)(2,1)} fusion(bf16[64,6144]{1,0:T(8,128)(2,1)} %param.17), kind=kLoop, calls=%fused_computation.46 | loop fusion | bytes 1572864 | tf_op jit(solution)/shard_map/reshape | solution.py:57
  8.8 0.0 copy-start.2
  8.8 0.0 copy-start.4
  8.9 0.0 all-gather.3.cloned.1.call-update
  8.9 0.0 copy-done.3
  8.9 0.1 copy.57
  9.0 0.1 copy.58
  9.1 0.1 reshape.152
  9.2 1.8 %gather_fusion.1 = bf16[24,64,128]{2,1,0:T(8,128)(2,1)S(1)} fusion(bf16[64,48,128]{2,0,1:T(8,128)(2,1)} %copy_bitcast_fusion, s32[1024]{0:T(1024)S(1)} %pad_clamp_fusion.1), kind=kCustom, calls=%fused_computation.1.clone | custom fusion | bytes 786528 | tf_op jit(solution)/shard_map/jit(_take)/gather | solution.py:21
  10.9 0.0 copy-done.5
  11.0 0.1 iota_compare_fusion
  11.0 0.9 bitcast_select_fusion.9
  11.9 7.3 %all-to-all-start = ((bf16[64,8,3,128]{3,0,2,1:T(8,128)(2,1)}), bf16[64,8,3,128]{3,0,2,1:T(8,128)(2,1)S(1)}, u32[]{:S(2)}, u32[]{:S(2)}) async-start(bf16[64,8,3,128]{3,0,2,1:T(8,128)(2,1)} %bitcast_select_fusion.9), calls=%async_computation | async-start | bytes 786432 | tf_op jit(solution)/shard_map/all_to_all | solution.py:23
  19.2 0.0 all-gather.5.cloned.1.call-start
  19.2 0.0 copy-done.2
  19.2 0.0 copy-done.4
  19.2 0.1 copy.52
  19.4 0.1 copy.56
  19.5 0.1 copy.53
  19.6 0.1 copy.55
  19.7 0.1 reshape.148
  19.8 0.1 copy.60
  19.9 0.1 reshape.156
  20.0 10.8 %all-to-all-done = bf16[64,8,3,128]{3,0,2,1:T(8,128)(2,1)S(1)} async-done(((bf16[64,8,3,128]{3,0,2,1:T(8,128)(2,1)}), bf16[64,8,3,128]{3,0,2,1:T(8,128)(2,1)S(1)}, u32[]{:S(2)}, u32[]{:S(2)}) %all-to-all-start) | async-done | bytes 393248 | tf_op jit(solution)/shard_map/all_to_all | solution.py:23
  30.8 0.8 gather_fusion.2
  31.7 4.3 %fusion.12 = f32[48,64,128,1]{2,1,3,0:T(8,128)} fusion(bf16[48,6,128,128]{3,2,1,0:T(8,128)(2,1)} %param.12, bf16[48,2,64,128]{3,2,1,0:T(8,128)(2,1)S(1)} %bitcast.84, pred[48,2]{1,0:T(8,128)(4,1)S(1)} %copy.56), kind=kOutput, calls=%fused_computation.20 | convolution fusion | flops 202113024 | bytes 6291552 | tf_op jit(solution)/shard_map/rjab,prjb->pra/dot_general | solution.py:52
  36.0 4.3 %all-gather.3.cloned.1.call-done = bf16[64,192,128]{2,0,1:T(8,128)(2,1)} async-done(((bf16[64,48,128]{2,0,1:T(8,128)(2,1)}), bf16[64,192,128]{2,0,1:T(8,128)(2,1)}) %all-gather.3.cloned.1.call-update) | async-done | bytes 3145744 | tf_op jit(solution)/shard_map/all_gather | solution.py:39
  40.3 3.0 %gather_fusion = bf16[192,64,128]{2,1,0:T(8,128)(2,1)S(1)} fusion(bf16[64,192,128]{2,0,1:T(8,128)(2,1)} %all-gather.3.cloned.1.call-done, s32[1024]{0:T(1024)S(1)} %pad_clamp_fusion.2), kind=kCustom, calls=%fused_computation.clone | custom fusion | bytes 6292224 | tf_op jit(solution)/shard_map/jit(_take)/gather | solution.py:44
  43.3 5.4 %fusion.36 = bf16[64,48,128]{2,0,1:T(8,128)(2,1)} fusion(f32[48,64,128,1]{2,1,3,0:T(8,128)} %fusion.12, bf16[48,6,128,128]{3,2,1,0:T(8,128)(2,1)} %param.12, bf16[48,4,64,128]{3,2,1,0:T(8,128)(2,1)S(1)} %bitcast.81, pred[48,4]{1,0:T(8,128)(4,1)S(1)} %copy.53, pred[48,4]{1,0:T(8,128)(4,1)S(1)} %copy.52), kind=kOutput, calls=%fused_computation.45 | convolution fusion | flops 406585344 | bytes 11796864 | tf_op jit(solution)/shard_map/rjab,prjb->pra/dot_general | solution.py:46
  48.8 0.0 all-gather.5.cloned.1.call-update
  48.8 1.8 %gather_fusion.4 = bf16[24,64,128]{2,1,0:T(8,128)(2,1)S(1)} fusion(bf16[64,48,128]{2,0,1:T(8,128)(2,1)} %fusion.36, s32[1024]{0:T(1024)S(1)} %pad_clamp_fusion.1), kind=kCustom, calls=%fused_computation.4.clone | custom fusion | bytes 786528 | tf_op jit(solution)/shard_map/jit(_take)/gather | solution.py:21
  50.6 0.1 bitcast_select_fusion.8
  50.7 17.8 %all_to_all.10 = bf16[64,8,3,128]{3,0,2,1:T(8,128)(2,1)S(1)} all-to-all(bf16[64,8,3,128]{3,0,2,1:T(8,128)(2,1)S(1)} %bitcast_select_fusion.8), channel_id=1, replica_groups=mesh['dom'=8,'grp'=4] {'dom'}, dimensions={1} | all-to-all | bytes 786432 | tf_op jit(solution)/shard_map/all_to_all | solution.py:23
  68.5 0.8 gather_fusion.5
  69.3 8.2 %all-gather.5.cloned.1.call-done = bf16[64,192,128]{2,0,1:T(8,128)(2,1)} async-done(((bf16[64,48,128]{2,0,1:T(8,128)(2,1)}), bf16[64,192,128]{2,0,1:T(8,128)(2,1)}) %all-gather.5.cloned.1.call-update) | async-done | bytes 3145744 | tf_op jit(solution)/shard_map/all_gather | solution.py:39
  77.5 4.6 %gather_fusion.3 = bf16[192,64,128]{2,1,0:T(8,128)(2,1)} fusion(bf16[64,192,128]{2,0,1:T(8,128)(2,1)} %all-gather.5.cloned.1.call-done, s32[1024]{0:T(1024)S(1)} %pad_clamp_fusion.2), kind=kCustom, calls=%fused_computation.3.clone | custom fusion | bytes 6292224 | tf_op jit(solution)/shard_map/jit(_take)/gather | solution.py:44
  82.1 5.0 %fusion = f32[48,64,128,1]{2,1,3,0:T(8,128)S(1)} fusion(bf16[48,6,128,128]{3,2,1,0:T(8,128)(2,1)} %param.12, bf16[48,4,64,128]{3,2,1,0:T(8,128)(2,1)} %bitcast.80, pred[48,4]{1,0:T(8,128)(4,1)S(1)} %copy.53, pred[48,4]{1,0:T(8,128)(4,1)S(1)} %copy.52), kind=kOutput, calls=%fused_computation.6 | convolution fusion | flops 405798912 | bytes 11010432 | tf_op jit(solution)/shard_map/rjab,prjb->pra/dot_general | solution.py:46
  87.2 0.0 copy-start
  87.2 0.0 copy-start.1
  87.2 3.3 %fusion.18 = f32[48,8,8,128]{3,2,1,0:T(8,128)S(1)} fusion(f32[48,64,128,1]{2,1,3,0:T(8,128)S(1)} %fusion, bf16[48,6,128,128]{3,2,1,0:T(8,128)(2,1)} %param.12, bf16[48,2,64,128]{3,2,1,0:T(8,128)(2,1)S(1)} %bitcast.79, pred[48,2]{1,0:T(8,128)(4,1)S(1)} %copy.56), kind=kOutput, calls=%fused_computation.31 | convolution fusion | flops 202899456 | bytes 7864416 | tf_op jit(solution)/shard_map/rjab,prjb->pra/dot_general | solution.py:52
  90.5 0.0 copy-done
  90.5 0.0 copy-done.1
  90.5 0.6 fusion.14
  91.1 0.7 pad_maximum_fusion
  (11 shorter events, 0.1 us)
Async XLA Ops:
  6.5 2.3 %copy-start.3 = (s32[1,1,8,3]{2,1,3,0:T(1,128)S(1)}, s32[1,1,8,3]{2,1,3,0:T(1,128)}, u32[]{:S(2)}) copy-start(s32[1,1,8,3]{2,1,3,0:T(1,128)} %param.15) | copy-start | bytes 292
  6.5 4.4 %copy-start.5 = (s32[1,1,8]{2,1,0:T(1,128)S(1)}, s32[1,1,8]{2,1,0:T(1,128)}, u32[]{:S(2)}) copy-start(s32[1,1,8]{2,1,0:T(1,128)} %param.16) | copy-start | bytes 100
  6.5 33.7 %all-gather.3.cloned.1.call-start = ((), (), s32[]{:S(2)}) async-start(), calls=%async_computation.2 | async-start | bytes 3932160 | tf_op jit(solution)/shard_map/all_gather | solution.py:39
  8.8 10.3 %copy-start.2 = (s32[48,4]{0,1:T(4,128)S(1)}, s32[48,4]{0,1:T(4,128)}, u32[]{:S(2)}) copy-start(s32[48,4]{0,1:T(4,128)} %param.13) | copy-start | bytes 2308
  8.8 10.4 %copy-start.4 = (s32[48,2]{0,1:T(2,128)S(1)}, s32[48,2]{0,1:T(2,128)}, u32[]{:S(2)}) copy-start(s32[48,2]{0,1:T(2,128)} %param.14) | copy-start | bytes 1156
  11.9 18.9 %all-to-all-start = ((bf16[64,8,3,128]{3,0,2,1:T(8,128)(2,1)}), bf16[64,8,3,128]{3,0,2,1:T(8,128)(2,1)S(1)}, u32[]{:S(2)}, u32[]{:S(2)}) async-start(bf16[64,8,3,128]{3,0,2,1:T(8,128)(2,1)} %bitcast_select_fusion.9), calls=%async_computation | async-start | bytes 786432 | tf_op jit(solution)/shard_map/all_to_all | solution.py:23
  19.2 58.3 %all-gather.5.cloned.1.call-start = ((), (), s32[]{:S(2)}) async-start(), calls=%async_computation.3 | async-start | bytes 3932160 | tf_op jit(solution)/shard_map/all_gather | solution.py:39
  87.2 3.3 %copy-start = (bf16[64,48,128]{2,0,1:T(8,128)(2,1)S(1)}, bf16[64,48,128]{2,0,1:T(8,128)(2,1)}, u32[]{:S(2)}) copy-start(bf16[64,48,128]{2,0,1:T(8,128)(2,1)} %fusion.36) | copy-start | bytes 2359300
  87.2 3.3 %copy-start.1 = (bf16[64,6144]{1,0:T(8,128)(2,1)S(1)}, bf16[64,6144]{1,0:T(8,128)(2,1)}, u32[]{:S(2)}) copy-start(bf16[64,6144]{1,0:T(8,128)(2,1)} %param.17) | copy-start | bytes 2359300
Sparse Core Ops, SparseCore 0:
  9.0 31.2 all-gather.2
  48.9 28.5 all-gather.4
where the time goes:
time: 99.1 us; the launch traced here: 98.7 us
  waiting for transfers between devices  23.3 us (24%)
  matrix products  18.1 us (18%)
  blocking collectives  17.8 us (18%)
  local copies, waits for them, and re-layouts  16.2 us (16%)
  between operations  13.6 us (14%)
  starting transfers between devices  7.29 us (7%)
  other arithmetic  2.43 us (2%)
    all_to_all x1, blocking collectives, send_boundary(): lax.all_to_all(outgoing, 'dom', split_axis=1, concat_axis=1, tiled=True)  17.8 us
    all_gather x2, waiting for transfers between devices, local_part(): piece = lax.all_gather(own, 'grp', axis=1, tiled=True)  12.4 us
    all_to_all x1, waiting for transfers between devices, send_boundary(): lax.all_to_all(outgoing, 'dom', split_axis=1, concat_axis=1, tiled=True)  10.8 us
    dot_general x2, matrix products, local_part(): jnp.einsum('rjab,prjb->pra', local_blocks, picked, preferred_element_type...  10.5 us
    gather x2, local copies, waits for them, and re-layouts, local_part(): chosen = jnp.take(piece, index, axis=1)  7.69 us
    dot_general x2, matrix products, remote_part(): jnp.einsum('rjab,prjb->pra', remote_blocks, picked, preferred_element_typ...  7.59 us
    all_to_all x1, starting transfers between devices, send_boundary(): lax.all_to_all(outgoing, 'dom', split_axis=1, concat_axis=1, tiled=True)  7.25 us
    gather x2, local copies, waits for them, and re-layouts, send_boundary(): outgoing = jnp.take(own, send_list, axis=1)  3.51 us
  transfers between devices with their start and end apart: 3, of which 3 were waited for; matrix products, arithmetic and copies ran while one was open for 12% of the time, Pallas kernels for 0%

commit v1 on v0

v1 whole, which is shorter than its diff:
```python
import functools
import math

import jax
import jax.numpy as jnp
from jax import lax
from jax.experimental import pallas as pl
from jax.experimental.pallas import tpu as pltpu
from jax.sharding import PartitionSpec as P

KMOM = 256
MESH = pl.DeviceIdType.MESH


def jackson(order, total):
    angle = math.pi / (total + 1)
    return (
        (total - order + 1) * math.cos(order * angle) + math.sin(order * angle) / math.tan(angle)
    ) / (total + 1)


def kernel(
    doms, lanes, chunks, scales,
    cols, refs, send_blocks, send_counts, probes, blocks, moments,
    weights, own_a, own_b, gathered_a, gathered_b, outgoing, received_a, received_b,
    load_sem, across_send, across_recv, pair_send, pair_recv, pass_send, pass_recv, edge_send, edge_recv,
):
    own, gathered, received = (own_a, own_b), (gathered_a, gathered_b), (received_a, received_b)
    rows, _, bs = own_a.shape
    local = cols.shape[0]
    remote = refs.shape[0]
    cap = send_blocks.shape[0]
    part = rows // chunks
    hops = lanes // 2 - 1
    d = lax.axis_index("dom")
    g = lax.axis_index("grp")
    pair = g + 1 - 2 * lax.rem(g, 2)

    def load(k):
        span = pl.ds(k * part, part)
        return pltpu.make_async_copy(blocks.at[span], weights.at[span], load_sem.at[k])

    barrier = pltpu.get_barrier_semaphore()
    for hop in range(1, lanes):
        pl.semaphore_signal(barrier, inc=1, device_id=(d, lax.rem(g + hop, lanes)), device_id_type=MESH)

    @pl.loop(1, doms)
    def _(k):
        pl.semaphore_signal(barrier, inc=1, device_id=(lax.rem(d + k, doms), g), device_id_type=MESH)

    for k in range(chunks):
        load(k).start()

    def across(phase, hop, k):
        to = lax.rem(g + 2 * hop, lanes)
        return pltpu.make_async_remote_copy(
            own[phase].at[pl.ds(k * part, part)],
            gathered[phase].at[pl.ds(g * rows + k * part, part)],
            across_send.at[phase, hop - 1, k], across_recv.at[phase, hop - 1, k],
            device_id=(d, to), device_id_type=MESH,
        )

    def to_pair(phase, k):
        return pltpu.make_async_remote_copy(
            own[phase].at[pl.ds(k * part, part)],
            gathered[phase].at[pl.ds(g * rows + k * part, part)],
            pair_send.at[phase, k], pair_recv.at[phase, k],
            device_id=(d, pair), device_id_type=MESH,
        )

    def pass_on(phase, hop, k):
        origin = lax.rem(g - 2 * hop + lanes, lanes)
        span = pl.ds(origin * rows + k * part, part)
        return pltpu.make_async_remote_copy(
            gathered[phase].at[span], gathered[phase].at[span],
            pass_send.at[phase, hop - 1, k], pass_recv.at[phase, hop - 1, k],
            device_id=(d, pair), device_id_type=MESH,
        )

    def edge(phase, k):
        to = lax.rem(d + k, doms)
        return pltpu.make_async_remote_copy(
            outgoing.at[phase, pl.ds(to * cap, cap)],
            received[phase].at[pl.ds(d * cap, cap)],
            edge_send.at[phase, k], edge_recv.at[phase, k],
            device_id=(to, g), device_id_type=MESH,
        )

    def send_chunk(phase, k):
        for hop in range(1, hops + 1):
            across(phase, hop, k).start()
        to_pair(phase, k).start()

    def send_edges(phase):
        def packed(to, s):
            block = own[phase][send_blocks[s, to]]
            return jnp.where(s < send_counts[0, to], block, jnp.zeros_like(block))

        @pl.loop(1, doms)
        def _(k):
            to = lax.rem(d + k, doms)
            for s in range(cap):
                outgoing[phase, to * cap + s] = packed(to, s)
            edge(phase, k).start()

        for s in range(cap):
            received[phase][d * cap + s] = packed(d, s)

    def finish_exchange(phase):
        for k in range(chunks):
            for hop in range(1, hops + 1):
                across(phase, hop, k).wait_recv()
                pass_on(phase, hop, k).start()
        for k in range(chunks):
            to_pair(phase, k).wait_recv()

        @pl.loop(1, doms)
        def _(k):
            edge(phase, k).wait_recv()

        for k in range(chunks):
            for hop in range(1, hops + 1):
                pass_on(phase, hop, k).wait_recv()

    def drain(phase):
        for k in range(chunks):
            for hop in range(1, hops + 1):
                across(phase, hop, k).wait_send()
                pass_on(phase, hop, k).wait_send()
            to_pair(phase, k).wait_send()

        @pl.loop(1, doms)
        def _(k):
            edge(phase, k).wait_send()

    def product(phase, r):
        picked = [gathered[phase][cols[j, r]] for j in range(local)]
        picked += [received[phase][refs[j, r]] for j in range(remote)]
        held = [weights[r, j] for j in range(local + remote)]
        return lax.dot_general(
            jnp.concatenate(picked, axis=1), jnp.concatenate(held, axis=1),
            (((1,), (1,)), ((), ())), preferred_element_type=jnp.float32,
        )

    for r in range(rows):
        block = probes[:, pl.ds(r * bs, bs)]
        own[0][r] = block
        gathered[0][g * rows + r] = block

    pl.semaphore_wait(barrier, lanes - 1 + doms - 1)
    for k in range(chunks):
        send_chunk(0, k)
    send_edges(0)

    for r in range(rows):
        base = own[0][r].astype(jnp.float32)
        moments[0:1, pl.ds(r * bs, bs)] = scales[0] * jnp.sum(base * base, axis=0, keepdims=True)
    for k in range(chunks):
        load(k).wait()
    finish_exchange(0)

    for k in range(chunks):
        def first_row(i, carry, k=k):
            r = k * part + i
            first = product(0, r).astype(jnp.bfloat16)
            own[1][r] = first
            gathered[1][g * rows + r] = first
            term = own[0][r].astype(jnp.float32) * first.astype(jnp.float32)
            moments[1:2, pl.ds(pl.multiple_of(r * bs, bs), bs)] = scales[1] * jnp.sum(term, axis=0, keepdims=True)
            return carry

        lax.fori_loop(0, part, first_row, 0, unroll=4)
        send_chunk(1, k)
    send_edges(1)
    finish_exchange(1)

    def second_row(r, carry):
        base = own[0][r].astype(jnp.float32)
        term = base * (2.0 * product(1, r) - base)
        moments[2:3, pl.ds(pl.multiple_of(r * bs, bs), bs)] = scales[2] * jnp.sum(term, axis=0, keepdims=True)
        return carry

    lax.fori_loop(0, rows, second_row, 0, unroll=4)
    drain(0)
    drain(1)


def solution(mesh):
    doms, lanes = mesh.shape["dom"], mesh.shape["grp"]

    def on_device(blocks, local_cols, remote_refs, send_blocks, send_counts, probes):
        count, nodes = probes.shape
        rows, _, bs, _ = blocks.shape
        cap = send_blocks.shape[3]
        norm = 1.0 / math.sqrt(count)
        scales = tuple((1.0 if k == 0 else 2.0) * jackson(k, KMOM) * norm for k in range(3))
        chunks = 4
        hops = lanes // 2 - 1
        dma = pltpu.SemaphoreType.DMA
        vmem = pl.BlockSpec(memory_space=pltpu.VMEM)
        smem = pl.BlockSpec(memory_space=pltpu.SMEM)
        return pl.pallas_call(
            functools.partial(kernel, doms, lanes, chunks, scales),
            out_shape=jax.ShapeDtypeStruct((3, nodes), jnp.float32),
            in_specs=[smem, smem, smem, smem, vmem, pl.BlockSpec(memory_space=pl.ANY)],
            out_specs=vmem,
            scratch_shapes=[
                pltpu.VMEM(blocks.shape, jnp.bfloat16),
                pltpu.VMEM((rows, count, bs), jnp.bfloat16),
                pltpu.VMEM((rows, count, bs), jnp.bfloat16),
                pltpu.VMEM((lanes * rows, count, bs), jnp.bfloat16),
                pltpu.VMEM((lanes * rows, count, bs), jnp.bfloat16),
                pltpu.VMEM((2, doms * cap, count, bs), jnp.bfloat16),
                pltpu.VMEM((doms * cap, count, bs), jnp.bfloat16),
                pltpu.VMEM((doms * cap, count, bs), jnp.bfloat16),
                dma((chunks,)),
                dma((2, hops, chunks)), dma((2, hops, chunks)),
                dma((2, chunks)), dma((2, chunks)),
                dma((2, hops, chunks)), dma((2, hops, chunks)),
                dma((2, doms)), dma((2, doms)),
            ],
            compiler_params=pltpu.CompilerParams(
                collective_id=0, has_side_effects=True, vmem_limit_bytes=48 * 2**20
            ),
        )(local_cols.T, remote_refs.T, send_blocks[0, 0].T, send_counts[0], probes, blocks)

    in_specs = (
        P(("dom", "grp"), None, None, None),
        P(("dom", "grp"), None),
        P(("dom", "grp"), None),
        P("dom", "grp", None, None),
        P("dom", "grp", None),
        P(None, ("dom", "grp")),
    )
    return jax.shard_map(
        on_device, mesh=mesh, in_specs=in_specs, out_specs=P(None, ("dom", "grp")), check_vma=False
    )
```

time: 99.1 us -> 56.7 us (0.57)
  Pallas kernels: 0 us -> 52 us
  waiting for transfers between devices: 23.3 us -> 0 us
  matrix products: 18.1 us -> 0 us
  blocking collectives: 17.8 us -> 0 us
  between operations: 13.6 us -> 0.01 us
  local copies, waits for them, and re-layouts: 16.2 us -> 4.47 us
  starting transfers between devices: 7.29 us -> 0 us
  other arithmetic: 2.43 us -> 0 us
    pallas_call x0 -> x1, Pallas kernels: none -> 52 us  [on_device(): pl.pallas_call(functools.partial(kernel, doms, lanes, chunks, scales), ou...]
    dot_general x4 -> x0, matrix products: 18.1 us -> none  [the longest x2 10.5 us: local_part(): jnp.einsum('rjab,prjb->pra', local_blocks, picked, preferred_element_type...]
    all_to_all x1 -> x0, blocking collectives: 17.8 us -> none  [send_boundary(): lax.all_to_all(outgoing, 'dom', split_axis=1, concat_axis=1, tiled=True)]
    gather x6 -> x0, local copies, waits for them, and re-layouts: 12.9 us -> none  [the longest x2 7.69 us: local_part(): chosen = jnp.take(piece, index, axis=1)]
    all_gather x2 -> x0, waiting for transfers between devices: 12.4 us -> none  [local_part(): piece = lax.all_gather(own, 'grp', axis=1, tiled=True)]
    all_to_all x1 -> x0, waiting for transfers between devices: 10.8 us -> none  [send_boundary(): lax.all_to_all(outgoing, 'dom', split_axis=1, concat_axis=1, tiled=True)]
    all_to_all x1 -> x0, starting transfers between devices: 7.25 us -> none  [send_boundary(): lax.all_to_all(outgoing, 'dom', split_axis=1, concat_axis=1, tiled=True)]
    unnamed x12 -> x10, local copies, waits for them, and re-layouts: 0.03 us -> 4.47 us
  transfers between devices with their start and end apart: 3 -> 0, of which waited for: 3 -> 0; matrix products, arithmetic and copies ran while one was open for 12% -> 0% of each run, Pallas kernels for 0% -> 0%
where the time goes in v1:
time: 56.7 us; the launch traced here: 56.5 us
  Pallas kernels  52 us (92%)
  local copies, waits for them, and re-layouts  4.47 us (8%)
    pallas_call x1, Pallas kernels, on_device(): pl.pallas_call(functools.partial(kernel, doms, lanes, chunks, scales), ou...  52 us
    unnamed x10, local copies, waits for them, and re-layouts  4.47 us

profile of v1, /device:TPU:0, one launch (start us, length us, event | category | flops | bytes accessed | tf_op | source)
XLA Modules:
  0.0 56.5 jit_solution(11241690257659276876)
XLA Ops:
  0.0 0.7 %copy.9 = s32[1,1,8,3]{2,3,1,0:T(4,128)S(1)} copy(s32[1,1,8,3]{2,1,3,0:T(1,128)} %param.9) | data formatting | bytes 192
  0.7 0.0 copy-start
  0.7 1.1 %copy-done = bf16[64,6144]{1,0:T(8,128)(2,1)S(1)} copy-done((bf16[64,6144]{1,0:T(8,128)(2,1)S(1)}, bf16[64,6144]{1,0:T(8,128)(2,1)}, u32[]{:S(2)}) %copy-start) | copy-done | bytes 786456
  1.8 0.0 copy-start.1
  1.8 0.7 %copy-done.1 = s32[48,4]{0,1:T(4,128)S(1)} copy-done((s32[48,4]{0,1:T(4,128)S(1)}, s32[48,4]{0,1:T(4,128)}, u32[]{:S(2)}) %copy-start.1) | copy-done | bytes 792
  2.5 0.0 copy-start.2
  2.5 0.7 %copy-done.2 = s32[48,2]{0,1:T(2,128)S(1)} copy-done((s32[48,2]{0,1:T(2,128)S(1)}, s32[48,2]{0,1:T(2,128)}, u32[]{:S(2)}) %copy-start.2) | copy-done | bytes 408
  3.2 0.0 copy-start.3
  3.2 0.7 %copy-done.3 = s32[1,1,8]{2,1,0:T(1,128)S(1)} copy-done((s32[1,1,8]{2,1,0:T(1,128)S(1)}, s32[1,1,8]{2,1,0:T(1,128)}, u32[]{:S(2)}) %copy-start.3) | copy-done | bytes 56
  3.8 52.0 %shard_map.64 = f32[3,6144]{1,0:T(4,128)S(1)} custom-call(s32[4,48]{1,0:T(4,128)S(1)} %bitcast.9, s32[2,48]{1,0:T(2,128)S(1)} %bitcast.10, s32[3,8]{1,0:T(4,128)S(1)} %bitcast.8, s32[1,8]{1,0:T(1,128)S(1)} %bitcast.11, bf16[64,6144]{1,0:T(8,128)(2,1)S(1)} %copy-done, bf16[48,6,128,128]{3,2,1,0:T(8,128)(2,1)} %blocks.1), custom_call_target="tpu_custom_call" | custom-call | tf_op jit(solution)/shard_map/pallas_call | solution.py:202
  55.9 0.6 %copy.11 = f32[3,6144]{1,0:T(4,128)} copy(f32[3,6144]{1,0:T(4,128)S(1)} %shard_map.64) | data formatting | bytes 147456
Async XLA Ops:
  0.7 1.1 %copy-start = (bf16[64,6144]{1,0:T(8,128)(2,1)S(1)}, bf16[64,6144]{1,0:T(8,128)(2,1)}, u32[]{:S(2)}) copy-start(bf16[64,6144]{1,0:T(8,128)(2,1)} %probes.1) | copy-start | bytes 2359300
  1.8 0.7 %copy-start.1 = (s32[48,4]{0,1:T(4,128)S(1)}, s32[48,4]{0,1:T(4,128)}, u32[]{:S(2)}) copy-start(s32[48,4]{0,1:T(4,128)} %param.7) | copy-start | bytes 2308
  2.5 0.7 %copy-start.2 = (s32[48,2]{0,1:T(2,128)S(1)}, s32[48,2]{0,1:T(2,128)}, u32[]{:S(2)}) copy-start(s32[48,2]{0,1:T(2,128)} %param.8) | copy-start | bytes 1156
  3.2 0.7 %copy-start.3 = (s32[1,1,8]{2,1,0:T(1,128)S(1)}, s32[1,1,8]{2,1,0:T(1,128)}, u32[]{:S(2)}) copy-start(s32[1,1,8]{2,1,0:T(1,128)} %param.10) | copy-start | bytes 100

commit v2 on v1

v2 whole, which is shorter than its diff:
```python
import functools
import math

import jax
import jax.numpy as jnp
from jax import lax
from jax.experimental import pallas as pl
from jax.experimental.pallas import tpu as pltpu
from jax.sharding import PartitionSpec as P

KMOM = 256
UNROLL = 4
MESH = pl.DeviceIdType.MESH


def jackson(order, total):
    angle = math.pi / (total + 1)
    return (
        (total - order + 1) * math.cos(order * angle) + math.sin(order * angle) / math.tan(angle)
    ) / (total + 1)


def kernel(
    doms, lanes, chunks, halves, scales,
    cols_hbm, refs_hbm, blocks_sent, counts_sent, probes_hbm, blocks, moments,
    weights, probes, cols, refs, send_blocks, send_counts, *rest,
):
    stages = 2 * halves
    own, gathered, outgoing, received = (rest[i * stages : (i + 1) * stages] for i in range(4))
    (index_sem, probe_sem, load_sem, across_send, across_recv, pair_send, pair_recv,
     pass_send, pass_recv, edge_send, edge_recv) = rest[4 * stages :]
    rows, count, bs = own[0].shape
    local = cols.shape[0]
    remote = refs.shape[0]
    cap = send_blocks.shape[0]
    part = rows // chunks
    hops = lanes // 2 - 1
    d = lax.axis_index("dom")
    g = lax.axis_index("grp")
    pair = g + 1 - 2 * lax.rem(g, 2)

    def load(k):
        span = pl.ds(k * part, part)
        return pltpu.make_async_copy(blocks.at[span], weights.at[span], load_sem.at[k])

    def load_probes(k):
        span = pl.ds(k * part * bs, part * bs)
        return pltpu.make_async_copy(probes_hbm.at[:, span], probes.at[:, span], probe_sem.at[k])

    index_loads = [
        pltpu.make_async_copy(source, target, index_sem.at[i])
        for i, (source, target) in enumerate(
            ((blocks_sent, send_blocks), (counts_sent, send_counts), (cols_hbm, cols), (refs_hbm, refs))
        )
    ]
    for k in range(chunks):
        load_probes(k).start()
    for copy in index_loads:
        copy.start()

    barrier = pltpu.get_barrier_semaphore()
    for hop in range(1, lanes):
        pl.semaphore_signal(barrier, inc=1, device_id=(d, lax.rem(g + hop, lanes)), device_id_type=MESH)

    @pl.loop(1, doms)
    def _(k):
        pl.semaphore_signal(barrier, inc=1, device_id=(lax.rem(d + k, doms), g), device_id_type=MESH)

    def across(stage, hop, k):
        to = lax.rem(g + 2 * hop, lanes)
        return pltpu.make_async_remote_copy(
            own[stage].at[pl.ds(k * part, part)],
            gathered[stage].at[pl.ds(g * rows + k * part, part)],
            across_send.at[stage, hop - 1, k], across_recv.at[stage, hop - 1, k],
            device_id=(d, to), device_id_type=MESH,
        )

    def to_pair(stage, k):
        return pltpu.make_async_remote_copy(
            own[stage].at[pl.ds(k * part, part)],
            gathered[stage].at[pl.ds(g * rows + k * part, part)],
            pair_send.at[stage, k], pair_recv.at[stage, k],
            device_id=(d, pair), device_id_type=MESH,
        )

    def pass_on(stage, hop, k):
        origin = lax.rem(g - 2 * hop + lanes, lanes)
        span = pl.ds(origin * rows + k * part, part)
        return pltpu.make_async_remote_copy(
            gathered[stage].at[span], gathered[stage].at[span],
            pass_send.at[stage, hop - 1, k], pass_recv.at[stage, hop - 1, k],
            device_id=(d, pair), device_id_type=MESH,
        )

    def edge(stage, k):
        to = lax.rem(d + k, doms)
        return pltpu.make_async_remote_copy(
            outgoing[stage].at[pl.ds(to * cap, cap)],
            received[stage].at[pl.ds(d * cap, cap)],
            edge_send.at[stage, k], edge_recv.at[stage, k],
            device_id=(to, g), device_id_type=MESH,
        )

    def send_across(stage, k):
        for hop in range(1, hops + 1):
            across(stage, hop, k).start()

    def send_edges(stage):
        def packed(to, s):
            block = own[stage][send_blocks[s, 0, to]]
            return jnp.where(s < send_counts[0, 0, to], block, jnp.zeros_like(block))

        @pl.loop(1, doms)
        def _(k):
            to = lax.rem(d + k, doms)
            for s in range(cap):
                outgoing[stage][to * cap + s] = packed(to, s)
            edge(stage, k).start()

        for s in range(cap):
            received[stage][d * cap + s] = packed(d, s)

    def finish_exchange(stage):
        for k in range(chunks):
            for hop in range(1, hops + 1):
                across(stage, hop, k).wait_recv()
                pass_on(stage, hop, k).start()
        for k in range(chunks):
            to_pair(stage, k).wait_recv()

        @pl.loop(1, doms)
        def _(k):
            edge(stage, k).wait_recv()

        for k in range(chunks):
            for hop in range(1, hops + 1):
                pass_on(stage, hop, k).wait_recv()

    def drain(stage):
        for k in range(chunks):
            for hop in range(1, hops + 1):
                across(stage, hop, k).wait_send()
                pass_on(stage, hop, k).wait_send()
            to_pair(stage, k).wait_send()

        @pl.loop(1, doms)
        def _(k):
            edge(stage, k).wait_send()

    def product(stage, r):
        picked = [gathered[stage][cols[j, r]] for j in range(local)]
        picked += [received[stage][refs[j, r]] for j in range(remote)]
        held = [weights[r, j] for j in range(local + remote)]
        return lax.dot_general(
            jnp.concatenate(picked, axis=1), jnp.concatenate(held, axis=1),
            (((1,), (1,)), ((), ())), preferred_element_type=jnp.float32,
        )

    def add_moment(order, half, r, term):
        at = pl.ds(pl.multiple_of(r * bs, bs), bs)
        total = scales[order] * jnp.sum(term, axis=0, keepdims=True)
        if half > 0:
            total = moments[order : order + 1, at] + total
        moments[order : order + 1, at] = total

    for k in range(chunks):
        load_probes(k).wait()
        for half in range(halves):
            for r in range(k * part, (k + 1) * part):
                block = probes[half * count : (half + 1) * count, r * bs : (r + 1) * bs]
                own[half][r] = block
                gathered[half][g * rows + r] = block
        if k == 0:
            pl.semaphore_wait(barrier, lanes - 1 + doms - 1)
        send_across(0, k)
    for half in range(1, halves):
        for k in range(chunks):
            send_across(half, k)
    for half in range(halves):
        for k in range(chunks):
            to_pair(half, k).start()
    for copy in index_loads:
        copy.wait()
    for half in range(halves):
        send_edges(half)
    for k in range(chunks):
        load(k).start()

    for half in range(halves):
        def zeroth_row(r, carry, half=half):
            base = own[half][r].astype(jnp.float32)
            add_moment(0, half, r, base * base)
            return carry

        lax.fori_loop(0, rows, zeroth_row, 0, unroll=4)
    for k in range(chunks):
        load(k).wait()

    for half in range(halves):
        finish_exchange(half)
        for k in range(chunks):
            def first_row(i, carry, half=half, k=k):
                r = k * part + i
                first = product(half, r).astype(jnp.bfloat16)
                own[halves + half][r] = first
                gathered[halves + half][g * rows + r] = first
                add_moment(1, half, r, own[half][r].astype(jnp.float32) * first.astype(jnp.float32))
                return carry

            lax.fori_loop(0, part, first_row, 0, unroll=UNROLL)
            send_across(halves + half, k)
            to_pair(halves + half, k).start()
        send_edges(halves + half)

    for half in range(halves):
        finish_exchange(halves + half)

        def second_row(r, carry, half=half):
            base = own[half][r].astype(jnp.float32)
            add_moment(2, half, r, base * (2.0 * product(halves + half, r) - base))
            return carry

        lax.fori_loop(0, rows, second_row, 0, unroll=UNROLL)
    for stage in range(stages):
        drain(stage)


def solution(mesh):
    doms, lanes = mesh.shape["dom"], mesh.shape["grp"]

    def on_device(blocks, local_cols, remote_refs, send_blocks, send_counts, probes):
        count, nodes = probes.shape
        rows, _, bs, _ = blocks.shape
        cap = send_blocks.shape[3]
        norm = 1.0 / math.sqrt(count)
        scales = tuple((1.0 if k == 0 else 2.0) * jackson(k, KMOM) * norm for k in range(3))
        chunks, halves = 4, 2
        stages = 2 * halves
        hops = lanes // 2 - 1
        piece = (count // halves, bs)
        dma = pltpu.SemaphoreType.DMA
        hbm = pl.BlockSpec(memory_space=pltpu.HBM)
        operands = (
            local_cols.T, remote_refs.T, send_blocks[0].transpose(2, 0, 1), send_counts, probes, blocks
        )
        return pl.pallas_call(
            functools.partial(kernel, doms, lanes, chunks, halves, scales),
            out_shape=jax.ShapeDtypeStruct((3, nodes), jnp.float32),
            in_specs=[hbm] * 6,
            out_specs=pl.BlockSpec(memory_space=pltpu.VMEM),
            scratch_shapes=[
                pltpu.VMEM(blocks.shape, jnp.bfloat16),
                pltpu.VMEM(probes.shape, jnp.bfloat16),
                *(pltpu.SMEM(operand.shape, jnp.int32) for operand in operands[:4]),
                *[pltpu.VMEM((rows, *piece), jnp.bfloat16)] * stages,
                *[pltpu.VMEM((lanes * rows, *piece), jnp.bfloat16)] * stages,
                *[pltpu.VMEM((doms * cap, *piece), jnp.bfloat16)] * stages,
                *[pltpu.VMEM((doms * cap, *piece), jnp.bfloat16)] * stages,
                dma((4,)), dma((chunks,)), dma((chunks,)),
                dma((stages, hops, chunks)), dma((stages, hops, chunks)),
                dma((stages, chunks)), dma((stages, chunks)),
                dma((stages, hops, chunks)), dma((stages, hops, chunks)),
                dma((stages, doms)), dma((stages, doms)),
            ],
            compiler_params=pltpu.CompilerParams(
                collective_id=0, has_side_effects=True, vmem_limit_bytes=60 * 2**20
            ),
        )(*operands)

    in_specs = (
        P(("dom", "grp"), None, None, None),
        P(("dom", "grp"), None),
        P(("dom", "grp"), None),
        P("dom", "grp", None, None),
        P("dom", "grp", None),
        P(None, ("dom", "grp")),
    )
    return jax.shard_map(
        on_device, mesh=mesh, in_specs=in_specs, out_specs=P(None, ("dom", "grp")), check_vma=False
    )
```

time: 56.7 us -> 51.2 us (0.903); the launches traced: 56.5 us -> 50.2 us
  Pallas kernels: 52 us -> 48.6 us
  local copies, waits for them, and re-layouts: 4.47 us -> 1.55 us
    pallas_call x1, Pallas kernels: 52 us -> 48.6 us  [on_device(): pl.pallas_call(functools.partial(kernel, doms, lanes, chunks, halves, sca...]
    unnamed x10 -> x1, local copies, waits for them, and re-layouts: 4.47 us -> 1.55 us
where the time goes in v2:
time: 51.2 us; the launch traced here: 50.2 us
  Pallas kernels  48.6 us (95%)
  local copies, waits for them, and re-layouts  1.55 us (3%)
    pallas_call x1, Pallas kernels, on_device(): pl.pallas_call(functools.partial(kernel, doms, lanes, chunks, halves, sca...  48.6 us
    unnamed x1, local copies, waits for them, and re-layouts  1.55 us

profile of v2, /device:TPU:0, one launch (start us, length us, event | category | flops | bytes accessed | tf_op | source)
XLA Modules:
  0.0 50.2 jit_solution(11109270218633230286)
XLA Ops:
  0.0 48.6 %shard_map.64 = f32[3,6144]{1,0:T(4,128)} custom-call(s32[4,48]{1,0:T(4,128)} %bitcast.5, s32[2,48]{1,0:T(2,128)} %bitcast.7, s32[3,1,8]{2,1,0:T(1,128)} %bitcast.6, s32[1,1,8]{2,1,0:T(1,128)} %counts_sent.1, bf16[64,6144]{1,0:T(8,128)(2,1)} %probes_hbm.1, bf16[48,6,128,128]{3,2,1,0:T(8,128)(2,1)} %blocks.1), custom_call_target="tpu_custom_call" | custom-call | tf_op jit(solution)/shard_map/pallas_call | solution.py:246
  48.6 1.6 %copy.8 = f32[3,6144]{1,0:T(4,128)} copy(f32[3,6144]{1,0:T(4,128)} %shard_map.64) | data formatting | bytes 147456

commit v3 on v2

--- a/solution.py
+++ b/solution.py
@@ -9,7 +9,7 @@
 from jax.sharding import PartitionSpec as P
 
 KMOM = 256
-UNROLL = 4
+UNROLL = 12
 MESH = pl.DeviceIdType.MESH
 
 
@@ -101,10 +101,6 @@
             device_id=(to, g), device_id_type=MESH,
         )
 
-    def send_across(stage, k):
-        for hop in range(1, hops + 1):
-            across(stage, hop, k).start()
-
     def send_edges(stage):
         def packed(to, s):
             block = own[stage][send_blocks[s, 0, to]]
@@ -120,11 +116,16 @@
         for s in range(cap):
             received[stage][d * cap + s] = packed(d, s)
 
+    def advance(stage, k):
+        for hop in range(1, hops + 1):
+            across(stage, hop, k).wait_send()
+            if stage + 1 < stages:
+                across(stage + 1, hop, k).start()
+        for hop in range(1, hops + 1):
+            across(stage, hop, k).wait_recv()
+            pass_on(stage, hop, k).start()
+
     def finish_exchange(stage):
-        for k in range(chunks):
-            for hop in range(1, hops + 1):
-                across(stage, hop, k).wait_recv()
-                pass_on(stage, hop, k).start()
         for k in range(chunks):
             to_pair(stage, k).wait_recv()
 
@@ -139,7 +140,6 @@
     def drain(stage):
         for k in range(chunks):
             for hop in range(1, hops + 1):
-                across(stage, hop, k).wait_send()
                 pass_on(stage, hop, k).wait_send()
             to_pair(stage, k).wait_send()
 
@@ -172,10 +172,8 @@
                 gathered[half][g * rows + r] = block
         if k == 0:
             pl.semaphore_wait(barrier, lanes - 1 + doms - 1)
-        send_across(0, k)
-    for half in range(1, halves):
-        for k in range(chunks):
-            send_across(half, k)
+        for hop in range(1, hops + 1):
+            across(0, hop, k).start()
     for half in range(halves):
         for k in range(chunks):
             to_pair(half, k).start()
@@ -195,6 +193,8 @@
         lax.fori_loop(0, rows, zeroth_row, 0, unroll=4)
     for k in range(chunks):
         load(k).wait()
+    for k in range(chunks):
+        advance(0, k)
 
     for half in range(halves):
         finish_exchange(half)
@@ -208,8 +208,8 @@
                 return carry
 
             lax.fori_loop(0, part, first_row, 0, unroll=UNROLL)
-            send_across(halves + half, k)
             to_pair(halves + half, k).start()
+            advance(half + 1, k)
         send_edges(halves + half)
 
     for half in range(halves):
@@ -220,7 +220,10 @@
             add_moment(2, half, r, base * (2.0 * product(halves + half, r) - base))
             return carry
 
-        lax.fori_loop(0, rows, second_row, 0, unroll=UNROLL)
+        for k in range(chunks):
+            lax.fori_loop(k * part, (k + 1) * part, second_row, 0, unroll=UNROLL)
+            if half + 1 < halves:
+                advance(halves + half + 1, k)
     for stage in range(stages):
         drain(stage)
 

time: 51.2 us -> 49.8 us (0.973)
  Pallas kernels: 48.6 us -> 47.3 us
    pallas_call x1, Pallas kernels: 48.6 us -> 47.3 us  [on_device(): pl.pallas_call(functools.partial(kernel, doms, lanes, chunks, halves, sca...]
where the time goes in v3:
time: 49.8 us; the launch traced here: 48.8 us
  Pallas kernels  47.3 us (95%)
  local copies, waits for them, and re-layouts  1.55 us (3%)
    pallas_call x1, Pallas kernels, on_device(): pl.pallas_call(functools.partial(kernel, doms, lanes, chunks, halves, sca...  47.3 us
    unnamed x1, local copies, waits for them, and re-layouts  1.55 us

profile of v3, /device:TPU:0, one launch (start us, length us, event | category | flops | bytes accessed | tf_op | source)
XLA Modules:
  0.0 48.8 jit_solution(14180672160655829373)
XLA Ops:
  0.0 47.3 %shard_map.64 = f32[3,6144]{1,0:T(4,128)} custom-call(s32[4,48]{1,0:T(4,128)} %bitcast.5, s32[2,48]{1,0:T(2,128)} %bitcast.7, s32[3,1,8]{2,1,0:T(1,128)} %bitcast.6, s32[1,1,8]{2,1,0:T(1,128)} %counts_sent.1, bf16[64,6144]{1,0:T(8,128)(2,1)} %probes_hbm.1, bf16[48,6,128,128]{3,2,1,0:T(8,128)(2,1)} %blocks.1), custom_call_target="tpu_custom_call" | custom-call | tf_op jit(solution)/shard_map/pallas_call | solution.py:249
  47.3 1.6 %copy.8 = f32[3,6144]{1,0:T(4,128)} copy(f32[3,6144]{1,0:T(4,128)} %shard_map.64) | data formatting | bytes 147456
